TPU v7x, 32 devices: a whole 2x2x4 slice. The times are simulated.
32 devices in a mesh: groups: 2 (over x), seq: 16 (over z, y, core).
Axes of the slice: x: 2, y: 2, z: 4, core: 2. Of those that a mesh axis runs over, the one named last changes fastest.
Arguments:
- queries: bfloat16 [8192, 4096], P(('groups', 'seq')), parts along dimension 0, may hold values from -6 to 6
- key_rows: bfloat16 [8192, 2048], P(('groups', 'seq')), parts along dimension 0, may hold values from -6 to 6
- value_matrix: bfloat16 [8192, 2048], P(('groups', 'seq')), parts along dimension 0, may hold values from -6 to 6
Outputs:
- attended: bfloat16 [8192, 4096], P(('groups', 'seq')), parts along dimension 0
There are 2 independent parts, one for each index of `groups`. A program takes and returns all parts, laid end to end along the dimension named above; each array names one. Nothing has to cross between parts.
All inputs are finite; a program needn't handle non-finite values.
Results may differ from a plain program's by a relative error of at most 0.0045.
Values may be sent and summed in bfloat16 or wider, within the bound.
A program may use at most 64 MiB of HBM per device.

v0:
```python
from functools import reduce

import jax
import jax.numpy as jnp
from jax import lax
from jax.sharding import PartitionSpec as P

QUERY_HEADS = 32
KEY_VALUE_HEADS = 16
HEAD_WIDTH = 128
WINDOW = 1024


score_scale = 168.0 ** (-0.5)
masked_value = -1e30


def passed_along(shard, axis, by):
    length = lax.axis_size(axis)
    pairs = [(i, i + by) for i in range(length) if 0 <= i + by < length]
    return lax.ppermute(shard, axis, pairs)


def visible_pairs(query_pos, key_pos):
    return (
        (key_pos[None, :] <= query_pos[:, None])
        & (key_pos[None, :] > query_pos[:, None] - WINDOW)
        & (key_pos[None, :] >= 0)
    )


def per_device(queries, key_rows, value_matrix):
    length = queries.shape[0]
    hops_back = (WINDOW - 1) // length + 1
    query_groups = QUERY_HEADS // KEY_VALUE_HEADS
    local_kv = jnp.stack([key_rows, value_matrix])
    arrived = [local_kv]
    moving = local_kv
    for hop_count in range(hops_back):
        moving = passed_along(moving, "seq", 1)
        arrived.append(moving)
    device = lax.axis_index("seq")
    offsets = jnp.arange(length, dtype=jnp.int32)
    query_pos = device * length + offsets
    visible_sets = [
        visible_pairs(query_pos, (device - hop_count) * length + offsets)
        for hop_count in range(hops_back + 1)
    ]

    def head_count_ratio(head_index, output):
        query_head = lax.dynamic_slice_in_dim(
            queries, head_index * query_groups * HEAD_WIDTH, query_groups * HEAD_WIDTH, 1
        ).reshape(length, query_groups, HEAD_WIDTH)
        score_list = []
        for hop_count in range(hops_back + 1):
            key_head = lax.dynamic_slice_in_dim(
                arrived[hop_count][0], head_index * HEAD_WIDTH, HEAD_WIDTH, 1
            )
            raw_scores = (
                jnp.einsum("tgd,kd->gtk", query_head, key_head, preferred_element_type=jnp.float32)
                * score_scale
            )
            score_list.append(jnp.where(visible_sets[hop_count][None], raw_scores, masked_value))
        row_max = reduce(jnp.maximum, [jnp.max(entry, axis=2) for entry in score_list])
        row_total = jnp.zeros(row_max.shape, jnp.float32)
        weighted = jnp.zeros((length, query_groups, HEAD_WIDTH), jnp.float32)
        for hop_count in range(hops_back + 1):
            weights_full = jnp.where(
                visible_sets[hop_count][None],
                jnp.exp(score_list[hop_count] - row_max[:, :, None]),
                0.0,
            )
            row_total = row_total + jnp.sum(weights_full, axis=2)
            value_head = lax.dynamic_slice_in_dim(
                arrived[hop_count][1], head_index * HEAD_WIDTH, HEAD_WIDTH, 1
            )
            weighted = weighted + jnp.einsum(
                "gtk,kd->tgd",
                weights_full.astype(jnp.bfloat16),
                value_head,
                preferred_element_type=jnp.float32,
            )
        result = weighted / jnp.transpose(row_total)[:, :, None]
        result = result.reshape(length, query_groups * HEAD_WIDTH).astype(jnp.bfloat16)
        return lax.dynamic_update_slice_in_dim(
            output, result, head_index * query_groups * HEAD_WIDTH, 1
        )

    return lax.fori_loop(
        0, KEY_VALUE_HEADS, head_count_ratio, jnp.zeros(queries.shape, jnp.bfloat16)
    )


def solution(mesh):
    return jax.shard_map(
        per_device,
        mesh=mesh,
        in_specs=(
            P(("groups", "seq"), None),
            P(("groups", "seq"), None),
            P(("groups", "seq"), None),
        ),
        out_specs=P(("groups", "seq"), None),
        check_vma=False,
    )
```

profile of v0, /device:TPU:24, one launch (start us, length us, event | category | flops | bytes accessed | tf_op | source)
XLA Modules:
  0.0 283.5 jit_solution(13030155471916844959)
XLA Ops:
  1.7 1.9 collective-permute-start
  3.7 26.3 %collective-permute-done = bf16[2,256,2048]{2,1,0:T(8,128)(2,1)S(1)} collective-permute-done((bf16[2,256,2048]{2,1,0:T(8,128)(2,1)S(1)}, bf16[2,256,2048]{2,1,0:T(8,128)(2,1)S(1)}, u32[]{:S(2)}, u32[]{:S(2)}) %collective-permute-start) | collective-permute-done | bytes 2097184 | tf_op jit(solution)/shard_map/ppermute | solution.py:21
  31.9 26.3 %collective-permute-done.1 = bf16[2,256,2048]{2,1,0:T(8,128)(2,1)S(1)} collective-permute-done((bf16[2,256,2048]{2,1,0:T(8,128)(2,1)S(1)}, bf16[2,256,2048]{2,1,0:T(8,128)(2,1)S(1)}, u32[]{:S(2)}, u32[]{:S(2)}) %collective-permute-start.1) | collective-permute-done | bytes 2097184 | tf_op jit(solution)/shard_map/ppermute | solution.py:21
  59.6 1.9 collective-permute-start.2
  61.5 26.4 %collective-permute-done.2 = bf16[2,256,2048]{2,1,0:T(8,128)(2,1)} collective-permute-done((bf16[2,256,2048]{2,1,0:T(8,128)(2,1)S(1)}, bf16[2,256,2048]{2,1,0:T(8,128)(2,1)}, u32[]{:S(2)}, u32[]{:S(2)}) %collective-permute-start.2) | collective-permute-done | bytes 2097184 | tf_op jit(solution)/shard_map/ppermute | solution.py:21
  87.9 1.9 collective-permute-start.3
  89.9 26.5 %collective-permute-done.3 = bf16[2,256,2048]{2,1,0:T(8,128)(2,1)} collective-permute-done((bf16[2,256,2048]{2,1,0:T(8,128)(2,1)}, bf16[2,256,2048]{2,1,0:T(8,128)(2,1)}, u32[]{:S(2)}, u32[]{:S(2)}) %collective-permute-start.3) | collective-permute-done | bytes 2097184 | tf_op jit(solution)/shard_map/ppermute | solution.py:21
  118.0 165.5 %while.17 = (s32[]{:T(128)}, bf16[256,4096]{1,0:T(8,128)(2,1)}, bf16[256,2048]{1,0:T(8,128)(2,1)}, bf16[256,2048]{1,0:T(8,128)(2,1)}, bf16[256,4096]{1,0:T(8,128...) while((s32[]{:T(128)}, bf16[256,4096]{1,0:T(8,128)(2,1)}, ...), condition=%wide.region_11.12_spmd.clone.clone, body=%wide.region_0.11_spmd.clone.clone.sunk | while | flops 343145472 | bytes 38995596 | solution.py:89
  119.7 2.9 %fusion.146 = (bf16[1,256,2048]{2,1,0:T(8,128)(2,1)S(1)}, bf16[1,256,2048]{2,1,0:T(8,128)(2,1)S(1)}, bf16[1,256,2048]{2,1,0:T(8,128)(2,1)S(1)}, bf16[1,256,2048]{2,1,0:T(8,128)(2,1)S(1)}) fusion(bf16[2,256,2048]{2,1,0:T(8,128)(2,1)} %get-tuple-element.820, bf16[2,256,2048]{2,1,0:T(8,128)(2,1)} %get-tuple-element.819), kind=kLoop, calls=%fused_computation.114.clone.1 | loop fusion | bytes 8388608 | tf_op jit(solution)/shard_map/while/body/eval_jaxpr/slice | solution.py:75
  130.0 2.9 %fusion.146 = (bf16[1,256,2048]{2,1,0:T(8,128)(2,1)S(1)}, bf16[1,256,2048]{2,1,0:T(8,128)(2,1)S(1)}, bf16[1,256,2048]{2,1,0:T(8,128)(2,1)S(1)}, bf16[1,256,2048]{2,1,0:T(8,128)(2,1)S(1)}) fusion(bf16[2,256,2048]{2,1,0:T(8,128)(2,1)} %get-tuple-element.820, bf16[2,256,2048]{2,1,0:T(8,128)(2,1)} %get-tuple-element.819), kind=kLoop, calls=%fused_computation.114.clone.1 | loop fusion | bytes 8388608 | tf_op jit(solution)/shard_map/while/body/eval_jaxpr/slice | solution.py:75
  140.4 2.9 %fusion.146 = (bf16[1,256,2048]{2,1,0:T(8,128)(2,1)S(1)}, bf16[1,256,2048]{2,1,0:T(8,128)(2,1)S(1)}, bf16[1,256,2048]{2,1,0:T(8,128)(2,1)S(1)}, bf16[1,256,2048]{2,1,0:T(8,128)(2,1)S(1)}) fusion(bf16[2,256,2048]{2,1,0:T(8,128)(2,1)} %get-tuple-element.820, bf16[2,256,2048]{2,1,0:T(8,128)(2,1)} %get-tuple-element.819), kind=kLoop, calls=%fused_computation.114.clone.1 | loop fusion | bytes 8388608 | tf_op jit(solution)/shard_map/while/body/eval_jaxpr/slice | solution.py:75
  150.7 2.9 %fusion.146 = (bf16[1,256,2048]{2,1,0:T(8,128)(2,1)S(1)}, bf16[1,256,2048]{2,1,0:T(8,128)(2,1)S(1)}, bf16[1,256,2048]{2,1,0:T(8,128)(2,1)S(1)}, bf16[1,256,2048]{2,1,0:T(8,128)(2,1)S(1)}) fusion(bf16[2,256,2048]{2,1,0:T(8,128)(2,1)} %get-tuple-element.820, bf16[2,256,2048]{2,1,0:T(8,128)(2,1)} %get-tuple-element.819), kind=kLoop, calls=%fused_computation.114.clone.1 | loop fusion | bytes 8388608 | tf_op jit(solution)/shard_map/while/body/eval_jaxpr/slice | solution.py:75
  161.0 2.9 %fusion.146 = (bf16[1,256,2048]{2,1,0:T(8,128)(2,1)S(1)}, bf16[1,256,2048]{2,1,0:T(8,128)(2,1)S(1)}, bf16[1,256,2048]{2,1,0:T(8,128)(2,1)S(1)}, bf16[1,256,2048]{2,1,0:T(8,128)(2,1)S(1)}) fusion(bf16[2,256,2048]{2,1,0:T(8,128)(2,1)} %get-tuple-element.820, bf16[2,256,2048]{2,1,0:T(8,128)(2,1)} %get-tuple-element.819), kind=kLoop, calls=%fused_computation.114.clone.1 | loop fusion | bytes 8388608 | tf_op jit(solution)/shard_map/while/body/eval_jaxpr/slice | solution.py:75
  171.4 2.9 %fusion.146 = (bf16[1,256,2048]{2,1,0:T(8,128)(2,1)S(1)}, bf16[1,256,2048]{2,1,0:T(8,128)(2,1)S(1)}, bf16[1,256,2048]{2,1,0:T(8,128)(2,1)S(1)}, bf16[1,256,2048]{2,1,0:T(8,128)(2,1)S(1)}) fusion(bf16[2,256,2048]{2,1,0:T(8,128)(2,1)} %get-tuple-element.820, bf16[2,256,2048]{2,1,0:T(8,128)(2,1)} %get-tuple-element.819), kind=kLoop, calls=%fused_computation.114.clone.1 | loop fusion | bytes 8388608 | tf_op jit(solution)/shard_map/while/body/eval_jaxpr/slice | solution.py:75
  181.7 2.9 %fusion.146 = (bf16[1,256,2048]{2,1,0:T(8,128)(2,1)S(1)}, bf16[1,256,2048]{2,1,0:T(8,128)(2,1)S(1)}, bf16[1,256,2048]{2,1,0:T(8,128)(2,1)S(1)}, bf16[1,256,2048]{2,1,0:T(8,128)(2,1)S(1)}) fusion(bf16[2,256,2048]{2,1,0:T(8,128)(2,1)} %get-tuple-element.820, bf16[2,256,2048]{2,1,0:T(8,128)(2,1)} %get-tuple-element.819), kind=kLoop, calls=%fused_computation.114.clone.1 | loop fusion | bytes 8388608 | tf_op jit(solution)/shard_map/while/body/eval_jaxpr/slice | solution.py:75
  192.1 2.9 %fusion.146 = (bf16[1,256,2048]{2,1,0:T(8,128)(2,1)S(1)}, bf16[1,256,2048]{2,1,0:T(8,128)(2,1)S(1)}, bf16[1,256,2048]{2,1,0:T(8,128)(2,1)S(1)}, bf16[1,256,2048]{2,1,0:T(8,128)(2,1)S(1)}) fusion(bf16[2,256,2048]{2,1,0:T(8,128)(2,1)} %get-tuple-element.820, bf16[2,256,2048]{2,1,0:T(8,128)(2,1)} %get-tuple-element.819), kind=kLoop, calls=%fused_computation.114.clone.1 | loop fusion | bytes 8388608 | tf_op jit(solution)/shard_map/while/body/eval_jaxpr/slice | solution.py:75
  202.4 2.9 %fusion.146 = (bf16[1,256,2048]{2,1,0:T(8,128)(2,1)S(1)}, bf16[1,256,2048]{2,1,0:T(8,128)(2,1)S(1)}, bf16[1,256,2048]{2,1,0:T(8,128)(2,1)S(1)}, bf16[1,256,2048]{2,1,0:T(8,128)(2,1)S(1)}) fusion(bf16[2,256,2048]{2,1,0:T(8,128)(2,1)} %get-tuple-element.820, bf16[2,256,2048]{2,1,0:T(8,128)(2,1)} %get-tuple-element.819), kind=kLoop, calls=%fused_computation.114.clone.1 | loop fusion | bytes 8388608 | tf_op jit(solution)/shard_map/while/body/eval_jaxpr/slice | solution.py:75
  212.7 2.9 %fusion.146 = (bf16[1,256,2048]{2,1,0:T(8,128)(2,1)S(1)}, bf16[1,256,2048]{2,1,0:T(8,128)(2,1)S(1)}, bf16[1,256,2048]{2,1,0:T(8,128)(2,1)S(1)}, bf16[1,256,2048]{2,1,0:T(8,128)(2,1)S(1)}) fusion(bf16[2,256,2048]{2,1,0:T(8,128)(2,1)} %get-tuple-element.820, bf16[2,256,2048]{2,1,0:T(8,128)(2,1)} %get-tuple-element.819), kind=kLoop, calls=%fused_computation.114.clone.1 | loop fusion | bytes 8388608 | tf_op jit(solution)/shard_map/while/body/eval_jaxpr/slice | solution.py:75
  223.1 2.9 %fusion.146 = (bf16[1,256,2048]{2,1,0:T(8,128)(2,1)S(1)}, bf16[1,256,2048]{2,1,0:T(8,128)(2,1)S(1)}, bf16[1,256,2048]{2,1,0:T(8,128)(2,1)S(1)}, bf16[1,256,2048]{2,1,0:T(8,128)(2,1)S(1)}) fusion(bf16[2,256,2048]{2,1,0:T(8,128)(2,1)} %get-tuple-element.820, bf16[2,256,2048]{2,1,0:T(8,128)(2,1)} %get-tuple-element.819), kind=kLoop, calls=%fused_computation.114.clone.1 | loop fusion | bytes 8388608 | tf_op jit(solution)/shard_map/while/body/eval_jaxpr/slice | solution.py:75
  233.4 2.9 %fusion.146 = (bf16[1,256,2048]{2,1,0:T(8,128)(2,1)S(1)}, bf16[1,256,2048]{2,1,0:T(8,128)(2,1)S(1)}, bf16[1,256,2048]{2,1,0:T(8,128)(2,1)S(1)}, bf16[1,256,2048]{2,1,0:T(8,128)(2,1)S(1)}) fusion(bf16[2,256,2048]{2,1,0:T(8,128)(2,1)} %get-tuple-element.820, bf16[2,256,2048]{2,1,0:T(8,128)(2,1)} %get-tuple-element.819), kind=kLoop, calls=%fused_computation.114.clone.1 | loop fusion | bytes 8388608 | tf_op jit(solution)/shard_map/while/body/eval_jaxpr/slice | solution.py:75
  243.8 2.9 %fusion.146 = (bf16[1,256,2048]{2,1,0:T(8,128)(2,1)S(1)}, bf16[1,256,2048]{2,1,0:T(8,128)(2,1)S(1)}, bf16[1,256,2048]{2,1,0:T(8,128)(2,1)S(1)}, bf16[1,256,2048]{2,1,0:T(8,128)(2,1)S(1)}) fusion(bf16[2,256,2048]{2,1,0:T(8,128)(2,1)} %get-tuple-element.820, bf16[2,256,2048]{2,1,0:T(8,128)(2,1)} %get-tuple-element.819), kind=kLoop, calls=%fused_computation.114.clone.1 | loop fusion | bytes 8388608 | tf_op jit(solution)/shard_map/while/body/eval_jaxpr/slice | solution.py:75
  254.1 2.9 %fusion.146 = (bf16[1,256,2048]{2,1,0:T(8,128)(2,1)S(1)}, bf16[1,256,2048]{2,1,0:T(8,128)(2,1)S(1)}, bf16[1,256,2048]{2,1,0:T(8,128)(2,1)S(1)}, bf16[1,256,2048]{2,1,0:T(8,128)(2,1)S(1)}) fusion(bf16[2,256,2048]{2,1,0:T(8,128)(2,1)} %get-tuple-element.820, bf16[2,256,2048]{2,1,0:T(8,128)(2,1)} %get-tuple-element.819), kind=kLoop, calls=%fused_computation.114.clone.1 | loop fusion | bytes 8388608 | tf_op jit(solution)/shard_map/while/body/eval_jaxpr/slice | solution.py:75
  264.4 2.9 %fusion.146 = (bf16[1,256,2048]{2,1,0:T(8,128)(2,1)S(1)}, bf16[1,256,2048]{2,1,0:T(8,128)(2,1)S(1)}, bf16[1,256,2048]{2,1,0:T(8,128)(2,1)S(1)}, bf16[1,256,2048]{2,1,0:T(8,128)(2,1)S(1)}) fusion(bf16[2,256,2048]{2,1,0:T(8,128)(2,1)} %get-tuple-element.820, bf16[2,256,2048]{2,1,0:T(8,128)(2,1)} %get-tuple-element.819), kind=kLoop, calls=%fused_computation.114.clone.1 | loop fusion | bytes 8388608 | tf_op jit(solution)/shard_map/while/body/eval_jaxpr/slice | solution.py:75
  274.8 2.9 %fusion.146 = (bf16[1,256,2048]{2,1,0:T(8,128)(2,1)S(1)}, bf16[1,256,2048]{2,1,0:T(8,128)(2,1)S(1)}, bf16[1,256,2048]{2,1,0:T(8,128)(2,1)S(1)}, bf16[1,256,2048]{2,1,0:T(8,128)(2,1)S(1)}) fusion(bf16[2,256,2048]{2,1,0:T(8,128)(2,1)} %get-tuple-element.820, bf16[2,256,2048]{2,1,0:T(8,128)(2,1)} %get-tuple-element.819), kind=kLoop, calls=%fused_computation.114.clone.1 | loop fusion | bytes 8388608 | tf_op jit(solution)/shard_map/while/body/eval_jaxpr/slice | solution.py:75
  (347 shorter events, 123.7 us)
Async XLA Ops:
  1.7 28.3 %collective-permute-start = (bf16[2,256,2048]{2,1,0:T(8,128)(2,1)S(1)}, bf16[2,256,2048]{2,1,0:T(8,128)(2,1)S(1)}, u32[]{:S(2)}, u32[]{:S(2)}) collective-permute-start(bf16[2,256,2048]{2,1,0:T(8,128)(2,1)S(1)} %pad_maximum_fusion), channel_id=1, source_target_pairs={{0,1},{1,2},{2,3},{3,4},{4,5},{5,6},{6,7},{7,8},{8,9},{9,10},{10,1... | collective-permute-start | bytes 6291464 | tf_op jit(solution)/shard_map/ppermute | solution.py:21
  30.0 28.2 %collective-permute-start.1 = (bf16[2,256,2048]{2,1,0:T(8,128)(2,1)S(1)}, bf16[2,256,2048]{2,1,0:T(8,128)(2,1)S(1)}, u32[]{:S(2)}, u32[]{:S(2)}) collective-permute-start(bf16[2,256,2048]{2,1,0:T(8,128)(2,1)S(1)} %collective-permute-done), channel_id=1, source_target_pairs={{0,1},{1,2},{2,3},{3,4},{4,5},{5,6},{6,7},{7,8},{8,9},{9,10},{10,1... | collective-permute-start | bytes 6291464 | tf_op jit(solution)/shard_map/ppermute | solution.py:21
  58.2 1.4 copy-start
  59.6 28.3 %collective-permute-start.2 = (bf16[2,256,2048]{2,1,0:T(8,128)(2,1)S(1)}, bf16[2,256,2048]{2,1,0:T(8,128)(2,1)}, u32[]{:S(2)}, u32[]{:S(2)}) collective-permute-start(bf16[2,256,2048]{2,1,0:T(8,128)(2,1)S(1)} %collective-permute-done.1), channel_id=1, source_target_pairs={{0,1},{1,2},{2,3},{3,4},{4,5},{5,6},{6,7},{7,8},{8,9},{9,10},{10,1... | collective-permute-start | bytes 6291464 | tf_op jit(solution)/shard_map/ppermute | solution.py:21
  87.9 28.6 %collective-permute-start.3 = (bf16[2,256,2048]{2,1,0:T(8,128)(2,1)}, bf16[2,256,2048]{2,1,0:T(8,128)(2,1)}, u32[]{:S(2)}, u32[]{:S(2)}) collective-permute-start(bf16[2,256,2048]{2,1,0:T(8,128)(2,1)} %collective-permute-done.2), channel_id=1, source_target_pairs={{0,1},{1,2},{2,3},{3,4},{4,5},{5,6},{6,7},{7,8},{8,9},{9,10},{10,1... | collective-permute-start | bytes 6291464 | tf_op jit(solution)/shard_map/ppermute | solution.py:21
  119.7 3.4 %copy-start.1 = (bf16[2,256,2048]{2,1,0:T(8,128)(2,1)S(1)}, bf16[2,256,2048]{2,1,0:T(8,128)(2,1)}, u32[]{:S(2)}) copy-start(bf16[2,256,2048]{2,1,0:T(8,128)(2,1)} %get-tuple-element.818) | copy-start | bytes 6291460 | tf_op jit(solution)/shard_map/while
  130.0 3.4 %copy-start.1 = (bf16[2,256,2048]{2,1,0:T(8,128)(2,1)S(1)}, bf16[2,256,2048]{2,1,0:T(8,128)(2,1)}, u32[]{:S(2)}) copy-start(bf16[2,256,2048]{2,1,0:T(8,128)(2,1)} %get-tuple-element.818) | copy-start | bytes 6291460 | tf_op jit(solution)/shard_map/while
  140.3 3.4 %copy-start.1 = (bf16[2,256,2048]{2,1,0:T(8,128)(2,1)S(1)}, bf16[2,256,2048]{2,1,0:T(8,128)(2,1)}, u32[]{:S(2)}) copy-start(bf16[2,256,2048]{2,1,0:T(8,128)(2,1)} %get-tuple-element.818) | copy-start | bytes 6291460 | tf_op jit(solution)/shard_map/while
  150.7 3.4 %copy-start.1 = (bf16[2,256,2048]{2,1,0:T(8,128)(2,1)S(1)}, bf16[2,256,2048]{2,1,0:T(8,128)(2,1)}, u32[]{:S(2)}) copy-start(bf16[2,256,2048]{2,1,0:T(8,128)(2,1)} %get-tuple-element.818) | copy-start | bytes 6291460 | tf_op jit(solution)/shard_map/while
  161.0 3.4 %copy-start.1 = (bf16[2,256,2048]{2,1,0:T(8,128)(2,1)S(1)}, bf16[2,256,2048]{2,1,0:T(8,128)(2,1)}, u32[]{:S(2)}) copy-start(bf16[2,256,2048]{2,1,0:T(8,128)(2,1)} %get-tuple-element.818) | copy-start | bytes 6291460 | tf_op jit(solution)/shard_map/while
  171.4 3.4 %copy-start.1 = (bf16[2,256,2048]{2,1,0:T(8,128)(2,1)S(1)}, bf16[2,256,2048]{2,1,0:T(8,128)(2,1)}, u32[]{:S(2)}) copy-start(bf16[2,256,2048]{2,1,0:T(8,128)(2,1)} %get-tuple-element.818) | copy-start | bytes 6291460 | tf_op jit(solution)/shard_map/while
  181.7 3.4 %copy-start.1 = (bf16[2,256,2048]{2,1,0:T(8,128)(2,1)S(1)}, bf16[2,256,2048]{2,1,0:T(8,128)(2,1)}, u32[]{:S(2)}) copy-start(bf16[2,256,2048]{2,1,0:T(8,128)(2,1)} %get-tuple-element.818) | copy-start | bytes 6291460 | tf_op jit(solution)/shard_map/while
  192.1 3.4 %copy-start.1 = (bf16[2,256,2048]{2,1,0:T(8,128)(2,1)S(1)}, bf16[2,256,2048]{2,1,0:T(8,128)(2,1)}, u32[]{:S(2)}) copy-start(bf16[2,256,2048]{2,1,0:T(8,128)(2,1)} %get-tuple-element.818) | copy-start | bytes 6291460 | tf_op jit(solution)/shard_map/while
  202.4 3.4 %copy-start.1 = (bf16[2,256,2048]{2,1,0:T(8,128)(2,1)S(1)}, bf16[2,256,2048]{2,1,0:T(8,128)(2,1)}, u32[]{:S(2)}) copy-start(bf16[2,256,2048]{2,1,0:T(8,128)(2,1)} %get-tuple-element.818) | copy-start | bytes 6291460 | tf_op jit(solution)/shard_map/while
  212.7 3.4 %copy-start.1 = (bf16[2,256,2048]{2,1,0:T(8,128)(2,1)S(1)}, bf16[2,256,2048]{2,1,0:T(8,128)(2,1)}, u32[]{:S(2)}) copy-start(bf16[2,256,2048]{2,1,0:T(8,128)(2,1)} %get-tuple-element.818) | copy-start | bytes 6291460 | tf_op jit(solution)/shard_map/while
  223.1 3.4 %copy-start.1 = (bf16[2,256,2048]{2,1,0:T(8,128)(2,1)S(1)}, bf16[2,256,2048]{2,1,0:T(8,128)(2,1)}, u32[]{:S(2)}) copy-start(bf16[2,256,2048]{2,1,0:T(8,128)(2,1)} %get-tuple-element.818) | copy-start | bytes 6291460 | tf_op jit(solution)/shard_map/while
  233.4 3.4 %copy-start.1 = (bf16[2,256,2048]{2,1,0:T(8,128)(2,1)S(1)}, bf16[2,256,2048]{2,1,0:T(8,128)(2,1)}, u32[]{:S(2)}) copy-start(bf16[2,256,2048]{2,1,0:T(8,128)(2,1)} %get-tuple-element.818) | copy-start | bytes 6291460 | tf_op jit(solution)/shard_map/while
  243.8 3.4 %copy-start.1 = (bf16[2,256,2048]{2,1,0:T(8,128)(2,1)S(1)}, bf16[2,256,2048]{2,1,0:T(8,128)(2,1)}, u32[]{:S(2)}) copy-start(bf16[2,256,2048]{2,1,0:T(8,128)(2,1)} %get-tuple-element.818) | copy-start | bytes 6291460 | tf_op jit(solution)/shard_map/while
  254.1 3.4 %copy-start.1 = (bf16[2,256,2048]{2,1,0:T(8,128)(2,1)S(1)}, bf16[2,256,2048]{2,1,0:T(8,128)(2,1)}, u32[]{:S(2)}) copy-start(bf16[2,256,2048]{2,1,0:T(8,128)(2,1)} %get-tuple-element.818) | copy-start | bytes 6291460 | tf_op jit(solution)/shard_map/while
  264.4 3.4 %copy-start.1 = (bf16[2,256,2048]{2,1,0:T(8,128)(2,1)S(1)}, bf16[2,256,2048]{2,1,0:T(8,128)(2,1)}, u32[]{:S(2)}) copy-start(bf16[2,256,2048]{2,1,0:T(8,128)(2,1)} %get-tuple-element.818) | copy-start | bytes 6291460 | tf_op jit(solution)/shard_map/while
  274.8 3.4 %copy-start.1 = (bf16[2,256,2048]{2,1,0:T(8,128)(2,1)S(1)}, bf16[2,256,2048]{2,1,0:T(8,128)(2,1)}, u32[]{:S(2)}) copy-start(bf16[2,256,2048]{2,1,0:T(8,128)(2,1)} %get-tuple-element.818) | copy-start | bytes 6291460 | tf_op jit(solution)/shard_map/while
where the time goes:
time: 285 us; the launch traced here: 284 us
  waiting for transfers between devices  106 us (37%)
  local copies, waits for them, and re-layouts  82.8 us (29%)
  matrix products  65.3 us (23%)
  other arithmetic  20 us (7%)
  starting transfers between devices  7.65 us (3%)
    ppermute x4, waiting for transfers between devices, passed_along(): return lax.ppermute(shard, axis, pairs)  106 us
    slice x32, local copies, waits for them, and re-layouts, head_count_ratio(): arrived[hop_count][1]  51.3 us
    dot_general x80, matrix products, head_count_ratio(): jnp.einsum('gtk,kd->tgd', weights_full.astype(jnp.bfloat16), value_head,...  33.7 us
    dot_general x80, matrix products, head_count_ratio(): jnp.einsum('tgd,kd->gtk', query_head, key_head, preferred_element_type=jn...  31.6 us
    dynamic_slice x32, local copies, waits for them, and re-layouts, head_count_ratio(): lax.dynamic_slice_in_dim(queries, head_index * query_groups * HEAD_WIDTH,...  16.2 us
    dynamic_update_slice x32, local copies, waits for them, and re-layouts, head_count_ratio(): lax.dynamic_update_slice_in_dim(output, result, head_index * query_groups...  12.3 us
    and x16, other arithmetic, visible_pairs(): (key_pos[None, :] <= query_pos[:, None]) & (key_pos[None, :] > query_pos[...  9.25 us
    reduce_sum x16, other arithmetic, head_count_ratio(): row_total = row_total + jnp.sum(weights_full, axis=2)  8.73 us
  transfers between devices with their start and end apart: 4, of which 4 were waited for; matrix products, arithmetic and copies ran while one was open for 0% of the time, Pallas kernels for 0%

commit v1 on v0

v1 whole, which is shorter than its diff:
```python
import functools
import math

import jax
import jax.numpy as jnp
from jax import lax
from jax.experimental import pallas as pl
from jax.experimental.pallas import tpu as pltpu
from jax.sharding import PartitionSpec as P

QUERY_HEADS = 32
KEY_VALUE_HEADS = 16
HEAD_WIDTH = 128
WINDOW = 1024

GROUP = QUERY_HEADS // KEY_VALUE_HEADS
HALF = 128
AHEAD = 4
EXPONENT = 168.0 ** (-0.5) * math.log2(math.e)
HIDDEN = 1e30


def kernel(
    n_seq, q_hbm, k_hbm, v_hbm, o_hbm,
    q_buf, k_buf, v_buf, o_buf, send_sem, recv_sem, q_sem, out_sem,
):
    rows = q_hbm.shape[0]
    chunks = k_buf.shape[0]
    reach = k_buf.shape[1] // rows - 1

    me = lax.axis_index("seq")
    place = me % 4
    odd = me % 2
    upper = place // 2
    sibling = me + 1 - 2 * odd
    across = me + 2 - 4 * upper
    has_prev = me >= 4
    has_next = me < n_seq - 4

    sources = (k_hbm, v_hbm)
    buffers = (k_buf, v_buf)

    def own(i, c):
        return sources[i].at[:, pl.ds(pl.multiple_of(c * HEAD_WIDTH, HEAD_WIDTH), HEAD_WIDTH)]

    def slot(i, c, hop):
        return buffers[i].at[c, pl.ds((reach - hop) * rows, rows), :]

    def send(i, c, source, hop, way, target):
        return pltpu.make_async_remote_copy(
            src_ref=source,
            dst_ref=slot(i, c, hop),
            send_sem=send_sem.at[way, c, i],
            recv_sem=recv_sem.at[hop, c, i],
            device_id={"seq": target},
            device_id_type=pl.DeviceIdType.MESH,
        )

    def own_copy(i, c):
        return pltpu.make_async_copy(own(i, c), slot(i, c, 0), recv_sem.at[0, c, i])

    def arrived(c, hop):
        for i in range(2):
            send(i, c, slot(i, c, hop), hop, 0, sibling).wait_recv()

    def out_copy(c):
        columns = pl.ds(pl.multiple_of(c * GROUP * HEAD_WIDTH, HEAD_WIDTH), GROUP * HEAD_WIDTH)
        return pltpu.make_async_copy(o_buf.at[:, columns], o_hbm.at[:, columns], out_sem.at[c])

    def send_own(c):
        @pl.when(has_next)
        def _():
            for i in range(2):
                send(i, c, own(i, c), 4, 0, me + 4).start()

        @pl.when(upper == 0)
        def _():
            for i in range(2):
                send(i, c, own(i, c), 2, 1, across).start()

        @pl.when(odd == 0)
        def _():
            for i in range(2):
                send(i, c, own(i, c), 1, 2, sibling).start()

        for i in range(2):
            own_copy(i, c).start()

    def relay_four(c):
        @pl.when(has_prev)
        def _():
            arrived(c, 4)

            @pl.when(upper == 1)
            def _():
                for i in range(2):
                    send(i, c, slot(i, c, 4), 2, 1, across).start()

            @pl.when(odd == 1)
            def _():
                for i in range(2):
                    send(i, c, slot(i, c, 4), 3, 2, sibling).start()

    def relay_two(c):
        @pl.when(me >= 2)
        def _():
            arrived(c, 2)

            @pl.when(odd == 0)
            def _():
                for i in range(2):
                    send(i, c, slot(i, c, 2), 3, 3, sibling).start()

            @pl.when(odd == 1)
            def _():
                for i in range(2):
                    send(i, c, slot(i, c, 2), 1, 3, sibling).start()

    def sent(c):
        def done(way):
            for i in range(2):
                send(i, c, slot(i, c, 0), 1, way, sibling).wait_send()

        @pl.when(has_next)
        def _():
            done(0)

        @pl.when(has_prev | (upper == 0))
        def _():
            done(1)

        @pl.when(has_prev | (odd == 0))
        def _():
            done(2)

        @pl.when(me >= 2)
        def _():
            done(3)

    lower = [jnp.where(me >= hop, 0.0, -HIDDEN).astype(jnp.float32) for hop in range(reach + 1)]

    def attend(c):
        @pl.when(me >= 1)
        def _():
            arrived(c, 1)

        @pl.when(me >= 3)
        def _():
            arrived(c, 3)

        for i in range(2):
            own_copy(i, c).wait()

        tile = (GROUP * HALF, HALF)
        query = lax.broadcasted_iota(jnp.int32, tile, 0) % HALF
        key = lax.broadcasted_iota(jnp.int32, tile, 1)
        for half in range(rows // HALF):
            low, size = half * HALF, rows * reach + HALF
            pieces = size // HALF
            hops = [reach - (low + piece * HALF) // rows for piece in range(pieces)]
            q_parts = [
                q_buf[
                    pl.ds(low, HALF),
                    pl.ds(pl.multiple_of((c * GROUP + g) * HEAD_WIDTH, HEAD_WIDTH), HEAD_WIDTH),
                ]
                for g in range(GROUP)
            ]
            q_tile = jnp.concatenate(q_parts, axis=0)
            scores = lax.dot_general(
                q_tile,
                k_buf[c, pl.ds(low, size), :],
                (((1,), (1,)), ((), ())),
                preferred_element_type=jnp.float32,
            )
            parts = [scores[:, piece * HALF : (piece + 1) * HALF] for piece in range(pieces)]
            parts[0] = jnp.where(key > query, parts[0], -HIDDEN)
            parts[-1] = jnp.where(key <= query, parts[-1], -HIDDEN)
            top = None
            for hop in range(reach + 1):
                here = None
                for piece in range(pieces):
                    if hops[piece] == hop:
                        here = parts[piece] if here is None else jnp.maximum(here, parts[piece])
                if hop > 0:
                    here = here + lower[hop]
                top = here if top is None else jnp.maximum(top, here)
            row_max = jnp.max(top, axis=1, keepdims=True) * EXPONENT
            shift = [row_max - lower[hop] if hop > 0 else row_max for hop in range(reach + 1)]
            total, weights = None, []
            for piece in range(pieces):
                full = jnp.exp2(parts[piece] * EXPONENT - shift[hops[piece]])
                total = full if total is None else total + full
                weights.append(full.astype(jnp.bfloat16))
            row_total = jnp.sum(total, axis=1, keepdims=True)
            weighted = jnp.dot(
                jnp.concatenate(weights, axis=1),
                v_buf[c, pl.ds(low, size), :],
                preferred_element_type=jnp.float32,
            )
            result = (weighted / row_total).astype(jnp.bfloat16)
            for g in range(GROUP):
                o_buf[
                    pl.ds(low, HALF),
                    pl.ds(pl.multiple_of((c * GROUP + g) * HEAD_WIDTH, HEAD_WIDTH), HEAD_WIDTH),
                ] = result[g * HALF : (g + 1) * HALF]
        out_copy(c).start()

    barrier = pltpu.get_barrier_semaphore()

    def greet(device):
        pl.semaphore_signal(
            barrier, inc=1, device_id={"seq": device}, device_id_type=pl.DeviceIdType.MESH
        )

    greet(sibling)
    greet(across)

    @pl.when(has_next)
    def _():
        greet(me + 4)

    @pl.when(has_prev)
    def _():
        greet(me - 4)

    q_copy = pltpu.make_async_copy(q_hbm, q_buf, q_sem)
    q_copy.start()

    pl.semaphore_wait(barrier, 2 + jnp.where(has_next, 1, 0) + jnp.where(has_prev, 1, 0))

    for c in range(min(AHEAD, chunks)):
        send_own(c)

    for hop in range(1, reach + 1):
        @pl.when(me < hop)
        def _(hop=hop):
            def clear(c, carry):
                for i in range(2):
                    buffers[i][c, pl.ds((reach - hop) * rows, rows), :] = jnp.zeros(
                        (rows, HEAD_WIDTH), jnp.bfloat16
                    )
                return carry

            lax.fori_loop(0, chunks, clear, 0)

    q_copy.wait()

    def step(j, carry):
        @pl.when(j + AHEAD < chunks)
        def _():
            send_own(j + AHEAD)

        @pl.when(j < chunks)
        def _():
            relay_four(j)

        @pl.when(j >= 2)
        def _():
            attend(j - 2)

        @pl.when((j >= 1) & (j <= chunks))
        def _():
            relay_two(j - 1)

        return carry

    lax.fori_loop(0, chunks + 2, step, 0)

    def finish(c, carry):
        sent(c)
        out_copy(c).wait()
        return carry

    lax.fori_loop(0, chunks, finish, 0)


def per_device(n_seq, queries, key_rows, value_matrix):
    rows = queries.shape[0]
    reach = (WINDOW - 1) // rows + 1
    chunks = KEY_VALUE_HEADS
    window = (chunks, (reach + 1) * rows, HEAD_WIDTH)
    pairs = QUERY_HEADS * rows * (WINDOW + HALF)
    return pl.pallas_call(
        functools.partial(kernel, n_seq),
        out_shape=jax.ShapeDtypeStruct(queries.shape, jnp.bfloat16),
        in_specs=[pl.BlockSpec(memory_space=pl.ANY)] * 3,
        out_specs=pl.BlockSpec(memory_space=pl.ANY),
        scratch_shapes=[
            pltpu.VMEM(queries.shape, jnp.bfloat16),
            pltpu.VMEM(window, jnp.bfloat16),
            pltpu.VMEM(window, jnp.bfloat16),
            pltpu.VMEM(queries.shape, jnp.bfloat16),
            pltpu.SemaphoreType.DMA((4, chunks, 2)),
            pltpu.SemaphoreType.DMA((reach + 1, chunks, 2)),
            pltpu.SemaphoreType.DMA,
            pltpu.SemaphoreType.DMA((chunks,)),
        ],
        compiler_params=pltpu.CompilerParams(
            collective_id=0, has_side_effects=True, vmem_limit_bytes=48 * 2**20
        ),
        cost_estimate=pl.CostEstimate(
            flops=4 * HEAD_WIDTH * pairs, bytes_accessed=16 * 2**20, transcendentals=pairs
        ),
    )(queries, key_rows, value_matrix)


def solution(mesh):
    spec = P(("groups", "seq"), None)
    return jax.shard_map(
        functools.partial(per_device, mesh.shape["seq"]),
        mesh=mesh,
        in_specs=(spec, spec, spec),
        out_specs=spec,
        check_vma=False,
    )
```

time: 285 us -> 63 us (0.22)
  waiting for transfers between devices: 106 us -> 0 us
  local copies, waits for them, and re-layouts: 82.8 us -> 3.77 us
  matrix products: 65.3 us -> 0 us
  Pallas kernels: 0 us -> 58.9 us
  other arithmetic: 20 us -> 0 us
  starting transfers between devices: 7.65 us -> 0 us
    ppermute x4 -> x0, waiting for transfers between devices: 106 us -> none  [passed_along(): return lax.ppermute(shard, axis, pairs)]
    dot_general x160 -> x0, matrix products: 65.3 us -> none  [the longest x80 33.7 us: head_count_ratio(): jnp.einsum('gtk,kd->tgd', weights_full.astype(jnp.bfloat16), value_head,...]
    pallas_call x0 -> x1, Pallas kernels: none -> 58.9 us  [per_device(): pl.pallas_call(functools.partial(kernel, n_seq), out_shape=jax.ShapeDtype...]
    slice x32 -> x0, local copies, waits for them, and re-layouts: 51.3 us -> none  [head_count_ratio(): arrived[hop_count][1]]
    dynamic_slice x32 -> x0, local copies, waits for them, and re-layouts: 16.2 us -> none  [head_count_ratio(): lax.dynamic_slice_in_dim(queries, head_index * query_groups * HEAD_WIDTH,...]
    dynamic_update_slice x32 -> x0, local copies, waits for them, and re-layouts: 12.3 us -> none  [head_count_ratio(): lax.dynamic_update_slice_in_dim(output, result, head_index * query_groups...]
    and x16 -> x0, other arithmetic: 9.25 us -> none  [visible_pairs(): (key_pos[None, :] <= query_pos[:, None]) & (key_pos[None, :] > query_pos[...]
    reduce_sum x16 -> x0, other arithmetic: 8.73 us -> none  [head_count_ratio(): row_total = row_total + jnp.sum(weights_full, axis=2)]
  transfers between devices with their start and end apart: 4 -> 0, of which waited for: 4 -> 0; matrix products, arithmetic and copies ran while one was open for 0% -> 0% of each run, Pallas kernels for 0% -> 0%
where the time goes in v1:
time: 63 us; the launch traced here: 62.7 us
  Pallas kernels  58.9 us (93%)
  local copies, waits for them, and re-layouts  3.77 us (6%)
    pallas_call x1, Pallas kernels, per_device(): pl.pallas_call(functools.partial(kernel, n_seq), out_shape=jax.ShapeDtype...  58.9 us
    unnamed x5, local copies, waits for them, and re-layouts  3.77 us

profile of v1, /device:TPU:24, one launch (start us, length us, event | category | flops | bytes accessed | tf_op | source)
XLA Modules:
  0.0 62.7 jit_solution(8175328327325826606)
XLA Ops:
  0.0 0.0 copy-start
  0.0 1.2 %copy-done = bf16[256,2048]{1,0:T(8,128)(2,1)S(1)} copy-done((bf16[256,2048]{1,0:T(8,128)(2,1)S(1)}, bf16[256,2048]{1,0:T(8,128)(2,1)}, u32[]{:S(2)}) %copy-start) | copy-done | bytes 1048600
  1.2 0.0 copy-start.1
  1.2 1.2 %copy-done.1 = bf16[256,2048]{1,0:T(8,128)(2,1)S(1)} copy-done((bf16[256,2048]{1,0:T(8,128)(2,1)S(1)}, bf16[256,2048]{1,0:T(8,128)(2,1)}, u32[]{:S(2)}) %copy-start.1) | copy-done | bytes 1048600
  2.5 58.9 %shard_map.37 = bf16[256,4096]{1,0:T(8,128)(2,1)S(1)} custom-call(bf16[256,4096]{1,0:T(8,128)(2,1)} %q_hbm.1, bf16[256,2048]{1,0:T(8,128)(2,1)S(1)} %copy-done, bf16[256,2048]{1,0:T(8,128)(2,1)S(1)} %copy-done.1), custom_call_target="tpu_custom_call" | custom-call | flops 4831838208 | bytes 16777216 | tf_op jit(solution)/shard_map/pallas_call | solution.py:283
  61.3 1.3 %copy.5 = bf16[256,4096]{1,0:T(8,128)(2,1)} copy(bf16[256,4096]{1,0:T(8,128)(2,1)S(1)} %shard_map.37) | data formatting | bytes 4194304
Async XLA Ops:
  0.0 1.2 %copy-start = (bf16[256,2048]{1,0:T(8,128)(2,1)S(1)}, bf16[256,2048]{1,0:T(8,128)(2,1)}, u32[]{:S(2)}) copy-start(bf16[256,2048]{1,0:T(8,128)(2,1)} %k_hbm.1) | copy-start | bytes 3145732
  1.2 1.2 %copy-start.1 = (bf16[256,2048]{1,0:T(8,128)(2,1)S(1)}, bf16[256,2048]{1,0:T(8,128)(2,1)}, u32[]{:S(2)}) copy-start(bf16[256,2048]{1,0:T(8,128)(2,1)} %v_hbm.1) | copy-start | bytes 3145732

commit v2 on v1

--- a/solution.py
+++ b/solution.py
@@ -59,9 +59,8 @@
     def own_copy(i, c):
         return pltpu.make_async_copy(own(i, c), slot(i, c, 0), recv_sem.at[0, c, i])
 
-    def arrived(c, hop):
-        for i in range(2):
-            send(i, c, slot(i, c, hop), hop, 0, sibling).wait_recv()
+    def arrived(i, c, hop):
+        send(i, c, slot(i, c, hop), hop, 0, sibling).wait_recv()
 
     def out_copy(c):
         columns = pl.ds(pl.multiple_of(c * GROUP * HEAD_WIDTH, HEAD_WIDTH), GROUP * HEAD_WIDTH)
@@ -86,35 +85,31 @@
         for i in range(2):
             own_copy(i, c).start()
 
-    def relay_four(c):
+    def relay_four(i, c):
         @pl.when(has_prev)
         def _():
-            arrived(c, 4)
+            arrived(i, c, 4)
 
             @pl.when(upper == 1)
             def _():
-                for i in range(2):
-                    send(i, c, slot(i, c, 4), 2, 1, across).start()
+                send(i, c, slot(i, c, 4), 2, 1, across).start()
 
             @pl.when(odd == 1)
             def _():
-                for i in range(2):
-                    send(i, c, slot(i, c, 4), 3, 2, sibling).start()
-
-    def relay_two(c):
+                send(i, c, slot(i, c, 4), 3, 2, sibling).start()
+
+    def relay_two(i, c):
         @pl.when(me >= 2)
         def _():
-            arrived(c, 2)
+            arrived(i, c, 2)
 
             @pl.when(odd == 0)
             def _():
-                for i in range(2):
-                    send(i, c, slot(i, c, 2), 3, 3, sibling).start()
+                send(i, c, slot(i, c, 2), 3, 3, sibling).start()
 
             @pl.when(odd == 1)
             def _():
-                for i in range(2):
-                    send(i, c, slot(i, c, 2), 1, 3, sibling).start()
+                send(i, c, slot(i, c, 2), 1, 3, sibling).start()
 
     def sent(c):
         def done(way):
@@ -139,18 +134,35 @@
 
     lower = [jnp.where(me >= hop, 0.0, -HIDDEN).astype(jnp.float32) for hop in range(reach + 1)]
 
-    def attend(c):
+    def complete(i, c):
         @pl.when(me >= 1)
         def _():
-            arrived(c, 1)
+            arrived(i, c, 1)
 
         @pl.when(me >= 3)
         def _():
-            arrived(c, 3)
-
-        for i in range(2):
-            own_copy(i, c).wait()
-
+            arrived(i, c, 3)
+
+        own_copy(i, c).wait()
+
+    def project(c, half, weights, row_total):
+        low, size = half * HALF, rows * reach + HALF
+        weighted = jnp.dot(
+            weights, v_buf[c, pl.ds(low, size), :], preferred_element_type=jnp.float32
+        )
+        result = (weighted / row_total).astype(jnp.bfloat16)
+        for g in range(GROUP):
+            o_buf[
+                pl.ds(low, HALF),
+                pl.ds(pl.multiple_of((c * GROUP + g) * HEAD_WIDTH, HEAD_WIDTH), HEAD_WIDTH),
+            ] = result[g * HALF : (g + 1) * HALF]
+
+    def attend(c, last=False):
+        complete(0, c)
+        if not last:
+            complete(1, c)
+
+        halves = []
         tile = (GROUP * HALF, HALF)
         query = lax.broadcasted_iota(jnp.int32, tile, 0) % HALF
         key = lax.broadcasted_iota(jnp.int32, tile, 1)
@@ -191,18 +203,15 @@
                 full = jnp.exp2(parts[piece] * EXPONENT - shift[hops[piece]])
                 total = full if total is None else total + full
                 weights.append(full.astype(jnp.bfloat16))
-            row_total = jnp.sum(total, axis=1, keepdims=True)
-            weighted = jnp.dot(
-                jnp.concatenate(weights, axis=1),
-                v_buf[c, pl.ds(low, size), :],
-                preferred_element_type=jnp.float32,
+            halves.append(
+                (jnp.concatenate(weights, axis=1), jnp.sum(total, axis=1, keepdims=True))
             )
-            result = (weighted / row_total).astype(jnp.bfloat16)
-            for g in range(GROUP):
-                o_buf[
-                    pl.ds(low, HALF),
-                    pl.ds(pl.multiple_of((c * GROUP + g) * HEAD_WIDTH, HEAD_WIDTH), HEAD_WIDTH),
-                ] = result[g * HALF : (g + 1) * HALF]
+            if not last:
+                project(c, half, *halves[half])
+        if last:
+            complete(1, c)
+            for half in range(rows // HALF):
+                project(c, half, *halves[half])
         out_copy(c).start()
 
     barrier = pltpu.get_barrier_semaphore()
@@ -250,21 +259,27 @@
         def _():
             send_own(j + AHEAD)
 
-        @pl.when(j < chunks)
-        def _():
-            relay_four(j)
-
-        @pl.when(j >= 2)
-        def _():
-            attend(j - 2)
-
-        @pl.when((j >= 1) & (j <= chunks))
-        def _():
-            relay_two(j - 1)
+        @pl.when(j >= 1)
+        def _():
+            relay_two(0, j - 1)
+            relay_two(1, j - 1)
+
+        relay_four(0, j)
+        relay_four(1, j)
+
+        @pl.when(j == chunks - 1)
+        def _():
+            relay_two(0, chunks - 1)
+
+        @pl.when(j >= 1)
+        def _():
+            attend(j - 1)
 
         return carry
 
-    lax.fori_loop(0, chunks + 2, step, 0)
+    lax.fori_loop(0, chunks, step, 0)
+    relay_two(1, chunks - 1)
+    attend(chunks - 1, last=True)
 
     def finish(c, carry):
         sent(c)
@@ -283,7 +298,7 @@
     return pl.pallas_call(
         functools.partial(kernel, n_seq),
         out_shape=jax.ShapeDtypeStruct(queries.shape, jnp.bfloat16),
-        in_specs=[pl.BlockSpec(memory_space=pl.ANY)] * 3,
+        in_specs=[pl.BlockSpec(memory_space=pltpu.HBM)] * 3,
         out_specs=pl.BlockSpec(memory_space=pl.ANY),
         scratch_shapes=[
             pltpu.VMEM(queries.shape, jnp.bfloat16),

time: 63 us -> 62.1 us (0.986)
  Pallas kernels: 58.9 us -> 57.6 us
    pallas_call x1, Pallas kernels: 58.9 us -> 57.6 us  [per_device(): pl.pallas_call(functools.partial(kernel, n_seq), out_shape=jax.ShapeDtype...]
where the time goes in v2:
time: 62.1 us; the launch traced here: 61.4 us
  Pallas kernels  57.6 us (93%)
  local copies, waits for them, and re-layouts  3.77 us (6%)
    pallas_call x1, Pallas kernels, per_device(): pl.pallas_call(functools.partial(kernel, n_seq), out_shape=jax.ShapeDtype...  57.6 us
    unnamed x5, local copies, waits for them, and re-layouts  3.77 us

profile of v2, /device:TPU:24, one launch (start us, length us, event | category | flops | bytes accessed | tf_op | source)
XLA Modules:
  0.0 61.4 jit_solution(8242106937826450883)
XLA Ops:
  0.0 0.0 copy-start
  0.0 1.2 %copy-done = bf16[256,2048]{1,0:T(8,128)(2,1)S(1)} copy-done((bf16[256,2048]{1,0:T(8,128)(2,1)S(1)}, bf16[256,2048]{1,0:T(8,128)(2,1)}, u32[]{:S(2)}) %copy-start) | copy-done | bytes 1048600
  1.2 0.0 copy-start.1
  1.2 1.2 %copy-done.1 = bf16[256,2048]{1,0:T(8,128)(2,1)S(1)} copy-done((bf16[256,2048]{1,0:T(8,128)(2,1)S(1)}, bf16[256,2048]{1,0:T(8,128)(2,1)}, u32[]{:S(2)}) %copy-start.1) | copy-done | bytes 1048600
  2.5 57.6 %shard_map.37 = bf16[256,4096]{1,0:T(8,128)(2,1)S(1)} custom-call(bf16[256,4096]{1,0:T(8,128)(2,1)} %q_hbm.1, bf16[256,2048]{1,0:T(8,128)(2,1)S(1)} %copy-done, bf16[256,2048]{1,0:T(8,128)(2,1)S(1)} %copy-done.1), custom_call_target="tpu_custom_call" | custom-call | flops 4831838208 | bytes 16777216 | tf_op jit(solution)/shard_map/pallas_call | solution.py:298
  60.1 1.3 %copy.5 = bf16[256,4096]{1,0:T(8,128)(2,1)} copy(bf16[256,4096]{1,0:T(8,128)(2,1)S(1)} %shard_map.37) | data formatting | bytes 4194304
Async XLA Ops:
  0.0 1.2 %copy-start = (bf16[256,2048]{1,0:T(8,128)(2,1)S(1)}, bf16[256,2048]{1,0:T(8,128)(2,1)}, u32[]{:S(2)}) copy-start(bf16[256,2048]{1,0:T(8,128)(2,1)} %k_hbm.1) | copy-start | bytes 3145732
  1.2 1.2 %copy-start.1 = (bf16[256,2048]{1,0:T(8,128)(2,1)S(1)}, bf16[256,2048]{1,0:T(8,128)(2,1)}, u32[]{:S(2)}) copy-start(bf16[256,2048]{1,0:T(8,128)(2,1)} %v_hbm.1) | copy-start | bytes 3145732

commit v3 on v2

--- a/solution.py
+++ b/solution.py
@@ -21,8 +21,8 @@
 
 
 def kernel(
-    n_seq, q_hbm, k_hbm, v_hbm, o_hbm,
-    q_buf, k_buf, v_buf, o_buf, send_sem, recv_sem, q_sem, out_sem,
+    n_seq, q_hbm, k_hbm, v_hbm, o_buf,
+    q_buf, k_buf, v_buf, send_sem, recv_sem, q_sem,
 ):
     rows = q_hbm.shape[0]
     chunks = k_buf.shape[0]
@@ -61,10 +61,6 @@
 
     def arrived(i, c, hop):
         send(i, c, slot(i, c, hop), hop, 0, sibling).wait_recv()
-
-    def out_copy(c):
-        columns = pl.ds(pl.multiple_of(c * GROUP * HEAD_WIDTH, HEAD_WIDTH), GROUP * HEAD_WIDTH)
-        return pltpu.make_async_copy(o_buf.at[:, columns], o_hbm.at[:, columns], out_sem.at[c])
 
     def send_own(c):
         @pl.when(has_next)
@@ -212,7 +208,6 @@
             complete(1, c)
             for half in range(rows // HALF):
                 project(c, half, *halves[half])
-        out_copy(c).start()
 
     barrier = pltpu.get_barrier_semaphore()
 
@@ -283,7 +278,6 @@
 
     def finish(c, carry):
         sent(c)
-        out_copy(c).wait()
         return carry
 
     lax.fori_loop(0, chunks, finish, 0)
@@ -297,21 +291,19 @@
     pairs = QUERY_HEADS * rows * (WINDOW + HALF)
     return pl.pallas_call(
         functools.partial(kernel, n_seq),
-        out_shape=jax.ShapeDtypeStruct(queries.shape, jnp.bfloat16),
+        out_shape=pltpu.VMEM(queries.shape, jnp.bfloat16),
         in_specs=[pl.BlockSpec(memory_space=pltpu.HBM)] * 3,
-        out_specs=pl.BlockSpec(memory_space=pl.ANY),
+        out_specs=pl.BlockSpec(memory_space=pltpu.VMEM),
         scratch_shapes=[
             pltpu.VMEM(queries.shape, jnp.bfloat16),
             pltpu.VMEM(window, jnp.bfloat16),
             pltpu.VMEM(window, jnp.bfloat16),
-            pltpu.VMEM(queries.shape, jnp.bfloat16),
             pltpu.SemaphoreType.DMA((4, chunks, 2)),
             pltpu.SemaphoreType.DMA((reach + 1, chunks, 2)),
             pltpu.SemaphoreType.DMA,
-            pltpu.SemaphoreType.DMA((chunks,)),
         ],
         compiler_params=pltpu.CompilerParams(
-            collective_id=0, has_side_effects=True, vmem_limit_bytes=48 * 2**20
+            collective_id=0, has_side_effects=True, vmem_limit_bytes=56 * 2**20
         ),
         cost_estimate=pl.CostEstimate(
             flops=4 * HEAD_WIDTH * pairs, bytes_accessed=16 * 2**20, transcendentals=pairs

time: 62.1 us -> 59.5 us (0.958)
  local copies, waits for them, and re-layouts: 3.77 us -> 1.32 us
    unnamed x5 -> x1, local copies, waits for them, and re-layouts: 3.77 us -> 1.32 us
where the time goes in v3:
time: 59.5 us; the launch traced here: 58.9 us
  Pallas kernels  57.6 us (97%)
  local copies, waits for them, and re-layouts  1.32 us (2%)
    pallas_call x1, Pallas kernels, per_device(): pl.pallas_call(functools.partial(kernel, n_seq), out_shape=pltpu.VMEM(que...  57.6 us
    unnamed x1, local copies, waits for them, and re-layouts  1.32 us

profile of v3, /device:TPU:24, one launch (start us, length us, event | category | flops | bytes accessed | tf_op | source)
XLA Modules:
  0.0 58.9 jit_solution(12287560617424457750)
XLA Ops:
  0.0 57.6 %shard_map.37 = bf16[256,4096]{1,0:T(8,128)(2,1)S(1)} custom-call(bf16[256,4096]{1,0:T(8,128)(2,1)} %q_hbm.1, bf16[256,2048]{1,0:T(8,128)(2,1)} %k_hbm.1, bf16[256,2048]{1,0:T(8,128)(2,1)} %v_hbm.1), custom_call_target="tpu_custom_call" | custom-call | flops 4831838208 | bytes 16777216 | tf_op jit(solution)/shard_map/pallas_call | solution.py:292
  57.6 1.3 %copy.5 = bf16[256,4096]{1,0:T(8,128)(2,1)} copy(bf16[256,4096]{1,0:T(8,128)(2,1)S(1)} %shard_map.37) | data formatting | bytes 4194304

commit v4 on v3

--- a/solution.py
+++ b/solution.py
@@ -15,6 +15,7 @@
 
 GROUP = QUERY_HEADS // KEY_VALUE_HEADS
 HALF = 128
+LAG = 4
 AHEAD = 4
 EXPONENT = 168.0 ** (-0.5) * math.log2(math.e)
 HIDDEN = 1e30
@@ -22,7 +23,7 @@
 
 def kernel(
     n_seq, q_hbm, k_hbm, v_hbm, o_buf,
-    q_buf, k_buf, v_buf, send_sem, recv_sem, q_sem,
+    q_buf, k_buf, v_buf, send_sem, recv_sem, q_sem, far_sem,
 ):
     rows = q_hbm.shape[0]
     chunks = k_buf.shape[0]
@@ -34,6 +35,7 @@
     upper = place // 2
     sibling = me + 1 - 2 * odd
     across = me + 2 - 4 * upper
+    diagonal = across + 1 - 2 * odd
     has_prev = me >= 4
     has_next = me < n_seq - 4
 
@@ -94,6 +96,25 @@
             def _():
                 send(i, c, slot(i, c, 4), 3, 2, sibling).start()
 
+    def far_copy(hop):
+        return pltpu.make_async_remote_copy(
+            src_ref=slot(1, chunks - 1, 4),
+            dst_ref=slot(1, chunks - 1, hop),
+            send_sem=far_sem,
+            recv_sem=recv_sem.at[hop, chunks - 1, 1],
+            device_id={"seq": diagonal},
+            device_id_type=pl.DeviceIdType.MESH,
+        )
+
+    def relay_far():
+        @pl.when(has_prev & (upper == 1) & (odd == 0))
+        def _():
+            far_copy(3).start()
+
+        @pl.when(has_prev & (upper == 1) & (odd == 1))
+        def _():
+            far_copy(1).start()
+
     def relay_two(i, c):
         @pl.when(me >= 2)
         def _():
@@ -126,7 +147,11 @@
 
         @pl.when(me >= 2)
         def _():
-            done(3)
+            send(0, c, slot(0, c, 0), 1, 3, sibling).wait_send()
+
+        @pl.when((me >= 2) & ((upper == 1) | (c < chunks - 1)))
+        def _():
+            send(1, c, slot(1, c, 0), 1, 3, sibling).wait_send()
 
     lower = [jnp.where(me >= hop, 0.0, -HIDDEN).astype(jnp.float32) for hop in range(reach + 1)]
 
@@ -206,6 +231,11 @@
                 project(c, half, *halves[half])
         if last:
             complete(1, c)
+
+            @pl.when(has_prev & (upper == 0))
+            def _():
+                arrived(1, c, 2)
+
             for half in range(rows // HALF):
                 project(c, half, *halves[half])
 
@@ -218,6 +248,7 @@
 
     greet(sibling)
     greet(across)
+    greet(diagonal)
 
     @pl.when(has_next)
     def _():
@@ -230,7 +261,7 @@
     q_copy = pltpu.make_async_copy(q_hbm, q_buf, q_sem)
     q_copy.start()
 
-    pl.semaphore_wait(barrier, 2 + jnp.where(has_next, 1, 0) + jnp.where(has_prev, 1, 0))
+    pl.semaphore_wait(barrier, 3 + jnp.where(has_next, 1, 0) + jnp.where(has_prev, 1, 0))
 
     for c in range(min(AHEAD, chunks)):
         send_own(c)
@@ -264,23 +295,36 @@
 
         @pl.when(j == chunks - 1)
         def _():
+            relay_far()
             relay_two(0, chunks - 1)
 
         @pl.when(j >= 1)
         def _():
             attend(j - 1)
 
+        @pl.when(j >= LAG)
+        def _():
+            sent(j - LAG)
+
         return carry
 
     lax.fori_loop(0, chunks, step, 0)
-    relay_two(1, chunks - 1)
+
+    @pl.when(upper == 1)
+    def _():
+        relay_two(1, chunks - 1)
+
     attend(chunks - 1, last=True)
 
     def finish(c, carry):
         sent(c)
         return carry
 
-    lax.fori_loop(0, chunks, finish, 0)
+    lax.fori_loop(chunks - LAG, chunks, finish, 0)
+
+    @pl.when(has_prev & (upper == 1))
+    def _():
+        far_copy(1).wait_send()
 
 
 def per_device(n_seq, queries, key_rows, value_matrix):
@@ -301,6 +345,7 @@
             pltpu.SemaphoreType.DMA((4, chunks, 2)),
             pltpu.SemaphoreType.DMA((reach + 1, chunks, 2)),
             pltpu.SemaphoreType.DMA,
+            pltpu.SemaphoreType.DMA,
         ],
         compiler_params=pltpu.CompilerParams(
             collective_id=0, has_side_effects=True, vmem_limit_bytes=56 * 2**20

time: 59.5 us -> 58.9 us (0.990)
  no operation moved by 1% of the time
where the time goes in v4:
time: 58.9 us; the launch traced here: 58.8 us
  Pallas kernels  57.4 us (97%)
  local copies, waits for them, and re-layouts  1.32 us (2%)
    pallas_call x1, Pallas kernels, per_device(): pl.pallas_call(functools.partial(kernel, n_seq), out_shape=pltpu.VMEM(que...  57.4 us
    unnamed x1, local copies, waits for them, and re-layouts  1.32 us

profile of v4, /device:TPU:24, one launch (start us, length us, event | category | flops | bytes accessed | tf_op | source)
XLA Modules:
  0.0 58.8 jit_solution(2227868070445202859)
XLA Ops:
  0.0 57.4 %shard_map.37 = bf16[256,4096]{1,0:T(8,128)(2,1)S(1)} custom-call(bf16[256,4096]{1,0:T(8,128)(2,1)} %q_hbm.1, bf16[256,2048]{1,0:T(8,128)(2,1)} %k_hbm.1, bf16[256,2048]{1,0:T(8,128)(2,1)} %v_hbm.1), custom_call_target="tpu_custom_call" | custom-call | flops 4831838208 | bytes 16777216 | tf_op jit(solution)/shard_map/pallas_call | solution.py:336
  57.4 1.3 %copy.5 = bf16[256,4096]{1,0:T(8,128)(2,1)} copy(bf16[256,4096]{1,0:T(8,128)(2,1)S(1)} %shard_map.37) | data formatting | bytes 4194304
